TPU v7x, 256 devices: a whole 4x4x8 slice. The times are simulated.
256 devices in a mesh: depth: 4 (over x), row: 8 (over z), col: 8 (over y, core).
Axes of the slice: x: 4, y: 4, z: 8, core: 2. Of those that a mesh axis runs over, the one named last changes fastest.
Arguments:
- inputs: bfloat16 [512, 12288], P('col', ('depth', 'row')), may hold values from -6 to 6
- w_in: bfloat16 [12288, 24576], P(('depth', 'row'), 'col'), may hold values from -0.0546875 to 0.0546875
- w_out: bfloat16 [24576, 12288], P('col', ('depth', 'row')), may hold values from -0.0390625 to 0.0390625
- grad_out: bfloat16 [512, 12288], P('col', ('depth', 'row')), may hold values from -1.5 to 1.5
Outputs:
- outputs: bfloat16 [512, 12288], P('col', ('depth', 'row'))
- input_grad: bfloat16 [512, 12288], P('col', ('depth', 'row'))
- grad_w_in: bfloat16 [12288, 24576], P(('depth', 'row'), 'col')
- grad_w_out: bfloat16 [24576, 12288], P('col', ('depth', 'row'))
All inputs are finite; a program needn't handle non-finite values.
Results may differ from a plain program's by a relative error of at most 0.019.
Values may be sent and summed in bfloat16 or wider, within the bound.
No kernel may reach another device: no remote copies, remote signals or barrier semaphores. Data moves between devices by JAX's collectives and lax.ppermute only.
A program may use at most 128 MiB of HBM per device.

v0:
```python
import jax
import jax.numpy as jnp
from jax import lax
from jax.sharding import PartitionSpec as P


def gelu_pair(pre):
    coeff = 0.7978845608
    inner = coeff * (pre + 0.044715 * pre * pre * pre)
    tval = jnp.tanh(inner)
    value = 0.5 * pre * (1.0 + tval)
    slope = 0.5 * (1.0 + tval) + 0.5 * pre * (1.0 - tval * tval) * coeff * (
        1.0 + 3.0 * 0.044715 * pre * pre
    )
    return (value, slope)


def activate(pre, back):
    value, slope = gelu_pair(pre)
    return (value.astype(jnp.bfloat16), (back * slope).astype(jnp.bfloat16))


def shards(inputs, w_in, w_out, grad_out):
    token_block, grad_block = (
        lax.all_gather(inputs, "col", axis=0, tiled=True),
        lax.all_gather(grad_out, "col", axis=0, tiled=True),
    )
    pre_part = jnp.dot(token_block, w_in, preferred_element_type=jnp.float32)
    back_part = lax.dot_general(
        grad_block, w_out, (((1,), (1,)), ((), ())), preferred_element_type=jnp.float32
    )
    pre_sum, back_sum = lax.psum((pre_part, back_part), ("depth", "row"))
    activated, hidden_grad = activate(pre_sum, back_sum)
    rows_now = activated
    outputs = lax.psum_scatter(
        jnp.dot(rows_now, w_out, preferred_element_type=jnp.float32).astype(jnp.bfloat16),
        "col",
        scatter_dimension=0,
        tiled=True,
    )
    rows_now = hidden_grad
    input_grad = lax.psum_scatter(
        lax.dot_general(
            rows_now, w_in, (((1,), (1,)), ((), ())), preferred_element_type=jnp.float32
        ).astype(jnp.bfloat16),
        "col",
        scatter_dimension=0,
        tiled=True,
    )
    grad_w_in = lax.dot_general(
        token_block, hidden_grad, (((0,), (0,)), ((), ())), preferred_element_type=jnp.float32
    ).astype(jnp.bfloat16)
    grad_w_out = lax.dot_general(
        activated, grad_block, (((0,), (0,)), ((), ())), preferred_element_type=jnp.float32
    ).astype(jnp.bfloat16)
    return (outputs, input_grad, grad_w_in, grad_w_out)


def solution(mesh):
    return jax.shard_map(
        shards,
        mesh=mesh,
        in_specs=(
            P("col", ("depth", "row")),
            P(("depth", "row"), "col"),
            P("col", ("depth", "row")),
            P("col", ("depth", "row")),
        ),
        out_specs=(
            P("col", ("depth", "row")),
            P("col", ("depth", "row")),
            P(("depth", "row"), "col"),
            P("col", ("depth", "row")),
        ),
        check_vma=False,
    )
```

profile of v0, /device:TPU:1, one launch (start us, length us, event | category | flops | bytes accessed | tf_op | source)
XLA Modules:
  0.0 398.9 jit_solution(16116521941050903696)
XLA Ops:
  7.2 0.0 copy-start
  7.2 0.0 all-reduce.3.cloned.1.call-start
  7.2 16.4 %all_gather.6 = bf16[512,384]{1,0:T(8,128)(2,1)S(1)} all-gather(bf16[64,384]{1,0:T(8,128)(2,1)} %param.4), channel_id=1, replica_groups=mesh['depth'=4,'row'=8,'col'=8] {'col'}, dimensions={0}, use_global_device_ids=true | all-gather | bytes 442368 | tf_op jit(solution)/shard_map/all_gather | solution.py:25
  23.6 13.2 %all_gather.7 = bf16[512,384]{1,0:T(8,128)(2,1)S(1)} all-gather(bf16[64,384]{1,0:T(8,128)(2,1)} %param.7), channel_id=1, replica_groups=mesh['depth'=4,'row'=8,'col'=8] {'col'}, dimensions={0}, use_global_device_ids=true | all-gather | bytes 442368 | tf_op jit(solution)/shard_map/all_gather | solution.py:26
  36.8 6.1 %fusion.9 = f32[512,3072]{1,0:T(8,128)} fusion(bf16[512,384]{1,0:T(8,128)(2,1)S(1)} %all_gather.7, bf16[3072,384]{1,0:T(8,128)(2,1)} %param.6), kind=kOutput, calls=%fused_computation.16 | convolution fusion | flops 1207959552 | bytes 9043968 | tf_op jit(solution)/shard_map/dot_general | solution.py:29
  42.9 0.0 copy-done
  42.9 4.4 %fusion.8 = f32[512,3072]{1,0:T(8,128)} fusion(bf16[512,384]{1,0:T(8,128)(2,1)S(1)} %all_gather.6, bf16[384,3072]{1,0:T(8,128)(2,1)S(1)} %copy-done), kind=kOutput, calls=%fused_computation.15 | convolution fusion | flops 1207959552 | bytes 9043968 | tf_op jit(solution)/shard_map/dot_general | solution.py:28
  47.3 0.0 all-reduce.3.cloned.1.call-update
  47.3 0.0 reduce-scatter.5.cloned.1.call-start
  47.3 266.5 %all-reduce.3.cloned.1.call-done = (f32[512,3072]{1,0:T(8,128)}, f32[512,3072]{1,0:T(8,128)}) async-done(((f32[512,3072]{1,0:T(8,128)}, f32[512,3072]{1,0:T(8,128)}), (f32[512,3072]{1,0:T(8,128)}, f32[512,3072]{1,0:T(8,128)})) %all-reduce.3.cloned.1.call-update) | async-done | bytes 12582928 | tf_op jit(solution)/shard_map/psum | solution.py:32
  313.8 6.8 %fusion.6 = bf16[512,3072]{1,0:T(8,128)(2,1)S(1)} fusion(f32[512,3072]{1,0:T(8,128)} %get-tuple-element.9, f32[512,3072]{1,0:T(8,128)} %get-tuple-element.8), kind=kLoop, calls=%fused_computation.8 | loop fusion | flops 29884416 | bytes 15728640 | tf_op jit(solution)/shard_map/convert_element_type | solution.py:20
  320.6 0.0 copy-start.1
  320.7 1.7 copy-done.1
  322.3 2.6 convolution_convert_fusion.2
  324.9 0.0 reduce-scatter.5.cloned.1.call-update
  324.9 0.2 reduce-scatter.3.cloned.1.call-start
  325.2 6.3 %convolution_convert_fusion.3 = bf16[512,384]{1,0:T(8,128)(2,1)} fusion(bf16[3072,384]{1,0:T(8,128)(2,1)} %param.6, f32[512,3072]{1,0:T(8,128)} %get-tuple-element.8), kind=kOutput, calls=%fused_computation.14 | convolution fusion | flops 1222311936 | bytes 9043968 | tf_op jit(solution)/shard_map/dot_general | solution.py:36
  331.5 0.0 reduce-scatter.3.cloned.1.call-update
  331.5 5.1 %fusion.7 = bf16[384,3072]{0,1:T(8,128)(2,1)} fusion(bf16[512,3072]{1,0:T(8,128)(2,1)} %copy-done.1, bf16[512,384]{1,0:T(8,128)(2,1)S(1)} %all_gather.6), kind=kOutput, calls=%fused_computation.12 | convolution fusion | flops 1209139200 | bytes 5898240 | tf_op jit(solution)/shard_map/dot_general | solution.py:50
  336.6 4.3 %copy.8 = bf16[384,3072]{1,0:T(8,128)(2,1)} copy(bf16[384,3072]{0,1:T(8,128)(2,1)} %fusion.7) | data formatting | bytes 4718592
  340.9 7.0 %convolution_convert_fusion = bf16[3072,384]{1,0:T(8,128)(2,1)} fusion(bf16[512,384]{1,0:T(8,128)(2,1)S(1)} %all_gather.7, f32[512,3072]{1,0:T(8,128)} %get-tuple-element.8), kind=kOutput, calls=%fused_computation.10 | convolution fusion | flops 1223294976 | bytes 9043968 | tf_op jit(solution)/shard_map/dot_general | solution.py:53
  347.9 9.0 %reduce-scatter.5.cloned.1.call-done = bf16[64,384]{1,0:T(8,128)(2,1)} async-done(((bf16[512,384]{1,0:T(8,128)(2,1)}), bf16[64,384]{1,0:T(8,128)(2,1)}) %reduce-scatter.5.cloned.1.call-update) | async-done | bytes 49168 | tf_op jit(solution)/shard_map/reduce_scatter | solution.py:42
  356.9 35.4 %reduce-scatter.3.cloned.1.call-done = bf16[64,384]{1,0:T(8,128)(2,1)} async-done(((bf16[512,384]{1,0:T(8,128)(2,1)}), bf16[64,384]{1,0:T(8,128)(2,1)}) %reduce-scatter.3.cloned.1.call-update) | async-done | bytes 49168 | tf_op jit(solution)/shard_map/reduce_scatter | solution.py:35
Async XLA Ops:
  7.2 35.7 %copy-start = (bf16[384,3072]{1,0:T(8,128)(2,1)S(1)}, bf16[384,3072]{1,0:T(8,128)(2,1)}, u32[]{:S(2)}) copy-start(bf16[384,3072]{1,0:T(8,128)(2,1)} %param.5) | copy-start | bytes 7077892
  7.2 306.6 %all-reduce.3.cloned.1.call-start = ((), (), s32[]{:S(2)}) async-start(), calls=%async_computation.4 | async-start | bytes 25165824 | tf_op jit(solution)/shard_map/psum | solution.py:32
  47.3 309.6 %reduce-scatter.5.cloned.1.call-start = ((), (), s32[]{:S(2)}) async-start(), calls=%async_computation.3 | async-start | bytes 442368 | tf_op jit(solution)/shard_map/reduce_scatter | solution.py:42
  320.6 1.7 copy-start.1
  324.9 67.4 %reduce-scatter.3.cloned.1.call-start = ((), (), s32[]{:S(2)}) async-start(), calls=%async_computation.2 | async-start | bytes 442368 | tf_op jit(solution)/shard_map/reduce_scatter | solution.py:35
Sparse Core Ops, SparseCore 0:
  47.4 266.3 all-reduce.2
  325.0 31.8 reduce-scatter.4
  360.2 32.1 reduce-scatter.2
where the time goes:
time: 401 us; the launch traced here: 399 us
  waiting for transfers between devices  311 us (78%)
  matrix products  31.5 us (8%)
  blocking collectives  29.6 us (7%)
  between operations  13.8 us (3%)
  other arithmetic  6.83 us (2%)
  local copies, waits for them, and re-layouts  5.98 us (1%)
    psum x1, waiting for transfers between devices, shards(): pre_sum, back_sum = lax.psum((pre_part, back_part), ('depth', 'row'))  266 us
    reduce_scatter x1, waiting for transfers between devices, shards(): lax.psum_scatter(jnp.dot(rows_now, w_out, preferred_element_type=jnp.floa...  35.4 us
    all_gather x1, blocking collectives, shards(): lax.all_gather(inputs, 'col', axis=0, tiled=True)  16.4 us
    all_gather x1, blocking collectives, shards(): lax.all_gather(grad_out, 'col', axis=0, tiled=True)  13.2 us
    reduce_scatter x1, waiting for transfers between devices, shards(): lax.psum_scatter(lax.dot_general(rows_now, w_in, (((1,), (1,)), ((), ()))...  9 us
  transfers between devices with their start and end apart: 3, of which 3 were waited for; matrix products, arithmetic and copies ran while one was open for 6% of the time, Pallas kernels for 0%

commit v1 on v0

v1 whole, which is shorter than its diff:
```python
import functools

import jax
import jax.numpy as jnp
import numpy as np
from jax import lax
from jax.experimental import pallas as pl
from jax.experimental.pallas import tpu as pltpu
from jax.sharding import PartitionSpec as P

BF = jnp.bfloat16
F32 = jnp.float32


def gelu_pair(pre):
    coeff = 0.7978845608
    inner = coeff * (pre + 0.044715 * pre * pre * pre)
    tval = jnp.tanh(inner)
    value = 0.5 * pre * (1.0 + tval)
    slope = 0.5 * (1.0 + tval) + 0.5 * pre * (1.0 - tval * tval) * coeff * (
        1.0 + 3.0 * 0.044715 * pre * pre
    )
    return (value, slope)


def shift_y(x, k):
    return lax.ppermute(x, "col", [(i, (i + 2 * k) % 8) for i in range(8)])


def swap_core(x):
    return lax.ppermute(x, "col", [(i, i ^ 1) for i in range(8)])


def together(pair):
    return lax.optimization_barrier(tuple(pair))


def add(x, y):
    return (x.astype(F32) + y.astype(F32)).astype(BF)


def after(x, *others):
    return lax.optimization_barrier((x,) + others)[0]


PAIRS_X = ([1, 0, 3, 2], [3, 2, 1, 0])
PAIRS_Z = ([1, 0, 3, 2, 5, 4, 7, 6], [7, 2, 1, 4, 3, 6, 5, 0], [3, 6, 5, 0, 7, 2, 1, 4])
STEPS = (
    (("x", 0), ("x", 1), ("z", 0), ("z", 1), ("z", 2)),
    (("z", 0), ("z", 1), ("x", 0), ("x", 1), ("z", 2)),
)


def ring_of(i, array, n):
    return i if array == 0 else (n - i) % n


def partner_of(d, r, core, step, array):
    axis, k = STEPS[core][step]
    if axis == "x":
        return ring_of(PAIRS_X[k][ring_of(d, array, 4)], array, 4), r
    return d, ring_of(PAIRS_Z[k][ring_of(r, array, 8)], array, 8)


def order_of(d, r, core, array, step):
    if step == 5:
        return [d * 8 + r]
    return order_of(*partner_of(d, r, core, step, array), core, array, step + 1) + order_of(
        d, r, core, array, step + 1
    )


def orders():
    return np.array(
        [
            [
                [[order_of(d, r, core, array, 0) for array in (0, 1)] for r in range(8)]
                for d in range(4)
            ]
            for core in (0, 1)
        ],
        np.int32,
    )


def exchange(x, step, array):
    pairs = []
    for d in range(4):
        for r in range(8):
            for c in range(8):
                d2, r2 = partner_of(d, r, c % 2, step, array)
                pairs.append((d * 64 + r * 8 + c, d2 * 64 + r2 * 8 + c))
    return lax.ppermute(x, ("depth", "row", "col"), pairs)


MIB = 1024 * 1024


def small(limit=8):
    return pltpu.CompilerParams(vmem_limit_bytes=limit * MIB)


VMEM = pl.BlockSpec(memory_space=pltpu.VMEM)


def pack(inputs, grad_out):
    feat = inputs.shape[1]

    def body(x_ref, g_ref, out_ref):
        out_ref[:, :feat] = x_ref[...]
        out_ref[:, feat:] = g_ref[...]

    return pl.pallas_call(
        body,
        out_shape=jax.ShapeDtypeStruct((inputs.shape[0], 2 * feat), BF),
        compiler_params=small(4),
    )(inputs, grad_out)


def partials(tok, array, piece, w_here, w_there):
    rows = tok.shape[0] // 2
    hid = w_here.shape[1 - array]
    step = 768

    def body(tok_ref, here_ref, there_ref, out_ref):
        now = tok_ref[piece * rows : (piece + 1) * rows, :]
        for base, ref in ((0, here_ref), (hid, there_ref)):
            for i in range(0, hid, step):
                if array == 0:
                    value = jnp.dot(now, ref[:, i : i + step], preferred_element_type=F32)
                else:
                    value = lax.dot_general(
                        ref[i : i + step, :], now, (((1,), (1,)), ((), ())), preferred_element_type=F32
                    ).T
                out_ref[:, base + i : base + i + step] = value.astype(BF)

    return pl.pallas_call(
        body,
        in_specs=[VMEM] * 3,
        out_specs=VMEM,
        out_shape=jax.ShapeDtypeStruct((rows, 2 * hid), BF),
        cost_estimate=pl.CostEstimate(
            flops=4 * rows * w_here.size, bytes_accessed=4 * rows * hid, transcendentals=0
        ),
        compiler_params=small(16),
    )(tok, w_here, w_there)


def products(act, hidden_grad, w_in, w_in2, w_out, w_out2):
    rows, hid = act.shape[0], w_in.shape[1]
    feat = w_in.shape[0]

    def body(a_ref, h_ref, in_ref, in2_ref, out_w_ref, out2_ref, out_ref):
        out_ref[0] = jnp.dot(a_ref[:, :hid], out_w_ref[...], preferred_element_type=F32) + jnp.dot(
            a_ref[:, hid:], out2_ref[...], preferred_element_type=F32
        )
        turned = (((1,), (1,)), ((), ()))
        out_ref[1] = (
            lax.dot_general(in_ref[...], h_ref[:, :hid], turned, preferred_element_type=F32)
            + lax.dot_general(in2_ref[...], h_ref[:, hid:], turned, preferred_element_type=F32)
        ).T

    return pl.pallas_call(
        body,
        in_specs=[VMEM] * 6,
        out_specs=VMEM,
        out_shape=jax.ShapeDtypeStruct((2, rows, feat), F32),
        cost_estimate=pl.CostEstimate(
            flops=8 * rows * w_in.size, bytes_accessed=8 * rows * hid, transcendentals=0
        ),
        compiler_params=small(24),
    )(act, hidden_grad, w_in, w_in2, w_out, w_out2)


def shards(inputs, w_in, w_out, grad_out):
    x_at, z_at = lax.axis_index("depth"), lax.axis_index("row")
    core = lax.rem(lax.axis_index("col"), 2)
    rows, feat = inputs.shape
    hid = w_in.shape[1]
    both = (0, 1)

    own = pack(inputs, grad_out)
    w_in2, w_out2 = swap_core(w_in), swap_core(w_out)
    tokens = jnp.concatenate([own] + [shift_y(own, -j) for j in (1, 2, 3)], axis=0)
    order = jnp.asarray(orders())[core, x_at, z_at]
    size = 4 * rows // 32
    wanted = (order[:, :, None] * size + jnp.arange(size, dtype=jnp.int32)).reshape(2, 4 * rows)
    pick = (wanted[:, :, None] == jnp.arange(4 * rows, dtype=jnp.int32)).astype(BF)
    ordered = [jnp.dot(pick[a], tokens, preferred_element_type=F32).astype(BF) for a in both]
    tok = (ordered[0][:, :feat], ordered[1][:, feat:])
    weights = ((w_in, w_in2), (w_out, w_out2))
    send = [partials(tok[a], a, 0, *weights[a]) for a in both]
    keep = [partials(tok[a], a, 1, *weights[a]) for a in both]

    for step in range(5):
        got = [exchange(send[a], step, a) for a in both]
        if step < 2:
            got = together(got)
        left = keep[0].shape[0] // 2
        if step == 4:
            total = [keep[a].astype(F32) + got[a] for a in both]
        else:
            send = [add(keep[a][:left], got[a][:left]) for a in both]
            keep = [keep[a][left:].astype(F32) + got[a][left:] for a in both]

    value, slope = gelu_pair(total[0])
    held = [value.astype(BF), (total[1] * slope).astype(BF)]

    for step in (4, 3, 2, 1, 0):
        got = [exchange(held[a], step, a) for a in both]
        if step < 2:
            got = together(got)
        if step == 0:
            two, rest = held, got
        else:
            held = [jnp.concatenate([got[a], held[a]], axis=0) for a in both]

    all_weights = (w_in, w_in2, w_out, w_out2)
    late, early = products(*rest, *all_weights), products(*two, *all_weights)
    out = [
        lax.dot_general(
            pick[a],
            jnp.concatenate([late[a], early[a]], axis=0).astype(BF),
            (((0,), (0,)), ((), ())),
            preferred_element_type=F32,
        ).astype(BF)
        for a in both
    ]
    out = jnp.stack(out)
    near_out = [shift_y(out[:, j * rows : (j + 1) * rows], j) for j in (1, 2, 3)]

    tok = jnp.stack([ordered[1][:, :feat], ordered[0][:, feat:]])
    tok2 = swap_core(tok)
    other_two = swap_core(jnp.stack([two[a][:, hid:] for a in both]))
    other_rest = swap_core(jnp.stack([rest[a][:, hid:] for a in both]))
    full = [
        jnp.concatenate([rest[a][:, :hid], two[a][:, :hid], other_rest[a], other_two[a]], axis=0)
        for a in both
    ]
    tokens = [jnp.concatenate([tok[k], tok2[k]], axis=0) for k in (0, 1)]

    def over_tokens(x, y):
        return lax.dot_general(x, y, (((0,), (0,)), ((), ())), preferred_element_type=F32).astype(BF)

    grads = (over_tokens(tokens[0], full[1]), over_tokens(full[0], tokens[1]))
    out, *grads = lax.optimization_barrier((out[:, :rows],) + grads)
    final = (out.astype(F32) + near_out[0] + near_out[1] + near_out[2]).astype(BF)
    return (final[0], final[1], *grads)


def solution(mesh):
    return jax.shard_map(
        shards,
        mesh=mesh,
        in_specs=(
            P("col", ("depth", "row")),
            P(("depth", "row"), "col"),
            P("col", ("depth", "row")),
            P("col", ("depth", "row")),
        ),
        out_specs=(
            P("col", ("depth", "row")),
            P("col", ("depth", "row")),
            P(("depth", "row"), "col"),
            P("col", ("depth", "row")),
        ),
        check_vma=False,
    )
```

time: 401 us -> 172 us (0.43)
  waiting for transfers between devices: 311 us -> 65.4 us
  starting transfers between devices: 0.3 us -> 74.9 us
  blocking collectives: 29.6 us -> 0 us
  matrix products: 31.5 us -> 6.86 us
  Pallas kernels: 0 us -> 16.1 us
  between operations: 13.8 us -> 1.07 us
    psum x1 -> x0, waiting for transfers between devices: 266 us -> none  [shards(): pre_sum, back_sum = lax.psum((pre_part, back_part), ('depth', 'row'))]
    ppermute x0 -> x31, starting transfers between devices: none -> 74.9 us  [the longest x5 33.1 us: swap_core(): return lax.ppermute(x, 'col', [(i, i ^ 1) for i in range(8)])]
    ppermute x0 -> x31, waiting for transfers between devices: none -> 65.4 us  [the longest x20 59.8 us: exchange(): return lax.ppermute(x, ('depth', 'row', 'col'), pairs)]
    reduce_scatter x2 -> x0, waiting for transfers between devices: 44.4 us -> none  [the longest x1 35.4 us: shards(): lax.psum_scatter(jnp.dot(rows_now, w_out, preferred_element_type=jnp.floa...]
    all_gather x2 -> x0, blocking collectives: 29.6 us -> none  [the longest x1 16.4 us: shards(): lax.all_gather(inputs, 'col', axis=0, tiled=True)]
    dot_general x6, matrix products: 31.5 us -> 6.86 us  [the longest x2 5.72 us: over_tokens(): lax.dot_general(x, y, (((0,), (0,)), ((), ())), preferred_element_type=F32)]
    pallas_call x0 -> x7, Pallas kernels: none -> 16.1 us  [the longest x4 8.24 us: partials(): pl.pallas_call(body, in_specs=[VMEM] * 3, out_specs=VMEM, out_shape=jax.S...]
    convert_element_type x1 -> x9, other arithmetic: 6.83 us -> 1.17 us  [the longest x7 0.91 us: add(): return (x.astype(F32) + y.astype(F32)).astype(BF)]
  transfers between devices with their start and end apart: 3 -> 31, of which waited for: 3 -> 23; matrix products, arithmetic and copies ran while one was open for 6% -> 6% of each run, Pallas kernels for 0% -> 9%
where the time goes in v1:
time: 172 us
  starting transfers between devices  74.9 us (44%)
  waiting for transfers between devices  65.4 us (38%)
  Pallas kernels  16.1 us (9%)
  matrix products  6.86 us (4%)
  local copies, waits for them, and re-layouts  4.82 us (3%)
  other arithmetic  2.95 us (2%)
    ppermute x20, waiting for transfers between devices, exchange(): return lax.ppermute(x, ('depth', 'row', 'col'), pairs)  59.8 us
    ppermute x5, starting transfers between devices, swap_core(): return lax.ppermute(x, 'col', [(i, i ^ 1) for i in range(8)])  33.1 us
    ppermute x20, starting transfers between devices, exchange(): return lax.ppermute(x, ('depth', 'row', 'col'), pairs)  33 us
    ppermute x6, starting transfers between devices, shift_y(): return lax.ppermute(x, 'col', [(i, (i + 2 * k) % 8) for i in range(8)])  8.77 us
    pallas_call x4, Pallas kernels, partials(): pl.pallas_call(body, in_specs=[VMEM] * 3, out_specs=VMEM, out_shape=jax.S...  8.24 us
    pallas_call x2, Pallas kernels, products(): pl.pallas_call(body, in_specs=[VMEM] * 6, out_specs=VMEM, out_shape=jax.S...  7.86 us
    dot_general x2, matrix products, over_tokens(): lax.dot_general(x, y, (((0,), (0,)), ((), ())), preferred_element_type=F32)  5.72 us
    ppermute x6, waiting for transfers between devices, shift_y(): return lax.ppermute(x, 'col', [(i, (i + 2 * k) % 8) for i in range(8)])  4.25 us
  transfers between devices with their start and end apart: 31, of which 23 were waited for; matrix products, arithmetic and copies ran while one was open for 6% of the time, Pallas kernels for 9%

profile of v1, /device:TPU:1, one launch (start us, length us, event | category | flops | bytes accessed | tf_op | source)
XLA Modules:
  0.0 172.1 jit_solution(1327566406349308576)
XLA Ops:
  0.6 3.3 %collective-permute-start.3 = (bf16[384,3072]{1,0:T(8,128)(2,1)}, bf16[384,3072]{1,0:T(8,128)(2,1)S(1)}, u32[]{:S(2)}, u32[]{:S(2)}) collective-permute-start(bf16[384,3072]{1,0:T(8,128)(2,1)} %in_ref.3), channel_id=1, source_target_pairs={{0,1},{1,0},{2,3},{3,2},{4,5},{5,4},{6,7},{7,6},{8,9},{9,8},{10,11... | collective-permute-start | bytes 7077896 | tf_op jit(solution)/shard_map/ppermute | solution.py:31
  17.2 3.1 %shard_map.87 = bf16[128,6144]{1,0:T(8,128)(2,1)S(1)} custom-call(bf16[256,384]{1,0:T(8,128)(2,1)S(1)} %get-tuple-element.59.tok_ref, bf16[3072,384]{1,0:T(8,128)(2,1)S(1)} %copy-done, bf16[3072,384]{1,0:T(8,128)(2,1)} %collective-permute-done.5.there_ref.out2_ref), custom_call_target="tpu_custom_call" | custom-call | flops 603979776 | bytes 1572864 | tf_op jit(solution)/shard_map/pallas_call | solution.py:137
  20.4 4.8 %collective-permute-start.6 = (bf16[128,6144]{1,0:T(8,128)(2,1)S(1)}, bf16[128,6144]{1,0:T(8,128)(2,1)S(1)}, u32[]{:S(2)}, u32[]{:S(2)}) collective-permute-start(bf16[128,6144]{1,0:T(8,128)(2,1)S(1)} %shard_map.87), channel_id=1, source_target_pairs={{0,192},{1,57},{2,194},{3,59},{4,196},{5,61},{6,198},{7,63},{8,200... | collective-permute-start | bytes 4718600 | tf_op jit(solution)/shard_map/ppermute | solution.py:93
  25.1 3.1 %shard_map.88 = bf16[128,6144]{1,0:T(8,128)(2,1)S(1)} custom-call(bf16[256,384]{1,0:T(8,128)(2,1)S(1)} %get-tuple-element.59.tok_ref, bf16[3072,384]{1,0:T(8,128)(2,1)S(1)} %copy-done, bf16[3072,384]{1,0:T(8,128)(2,1)} %collective-permute-done.5.there_ref.out2_ref), custom_call_target="tpu_custom_call" | custom-call | flops 603979776 | bytes 1572864 | tf_op jit(solution)/shard_map/pallas_call | solution.py:137
  29.3 6.6 %collective-permute-done.4 = bf16[128,6144]{1,0:T(8,128)(2,1)S(1)} collective-permute-done((bf16[128,6144]{1,0:T(8,128)(2,1)S(1)}, bf16[128,6144]{1,0:T(8,128)(2,1)S(1)}, u32[]{:S(2)}, u32[]{:S(2)}) %collective-permute-start.4) | collective-permute-done | bytes 1572896 | tf_op jit(solution)/shard_map/ppermute | solution.py:93
  35.9 7.1 %collective-permute-done.6 = bf16[128,6144]{1,0:T(8,128)(2,1)S(1)} collective-permute-done((bf16[128,6144]{1,0:T(8,128)(2,1)S(1)}, bf16[128,6144]{1,0:T(8,128)(2,1)S(1)}, u32[]{:S(2)}, u32[]{:S(2)}) %collective-permute-start.6) | collective-permute-done | bytes 1572896 | tf_op jit(solution)/shard_map/ppermute | solution.py:93
  43.3 3.0 %collective-permute-start.7 = (bf16[64,6144]{1,0:T(8,128)(2,1)S(1)}, bf16[64,6144]{1,0:T(8,128)(2,1)S(1)}, u32[]{:S(2)}, u32[]{:S(2)}) collective-permute-start(bf16[64,6144]{1,0:T(8,128)(2,1)S(1)} %get-tuple-element.28), channel_id=1, source_target_pairs={{0,192},{1,57},{2,194},{3,59},{4,196},{5,61},{6,198},{7,63},{8,200... | collective-permute-start | bytes 2359304 | tf_op jit(solution)/shard_map/ppermute | solution.py:93
  46.8 9.2 %collective-permute-done.7 = bf16[64,6144]{1,0:T(8,128)(2,1)S(1)} collective-permute-done((bf16[64,6144]{1,0:T(8,128)(2,1)S(1)}, bf16[64,6144]{1,0:T(8,128)(2,1)S(1)}, u32[]{:S(2)}, u32[]{:S(2)}) %collective-permute-start.7) | collective-permute-done | bytes 786464 | tf_op jit(solution)/shard_map/ppermute | solution.py:93
  60.8 5.5 %collective-permute-done.16 = bf16[32,6144]{1,0:T(8,128)(2,1)S(1)} collective-permute-done((bf16[32,6144]{1,0:T(8,128)(2,1)S(1)}, bf16[32,6144]{1,0:T(8,128)(2,1)S(1)}, u32[]{:S(2)}, u32[]{:S(2)}) %collective-permute-start.16) | collective-permute-done | bytes 393248 | tf_op jit(solution)/shard_map/ppermute | solution.py:93
  75.7 5.2 %collective-permute-done.18 = bf16[8,6144]{1,0:T(8,128)(2,1)S(1)} collective-permute-done((bf16[8,6144]{1,0:T(8,128)(2,1)S(1)}, bf16[8,6144]{1,0:T(8,128)(2,1)S(1)}, u32[]{:S(2)}, u32[]{:S(2)}) %collective-permute-start.18) | collective-permute-done | bytes 98336 | tf_op jit(solution)/shard_map/ppermute | solution.py:93
  82.8 3.6 %collective-permute-start.19 = (bf16[8,6144]{1,0:T(8,128)(2,1)S(1)}, bf16[8,6144]{1,0:T(8,128)(2,1)S(1)}, u32[]{:S(2)}, u32[]{:S(2)}) collective-permute-start(bf16[8,6144]{1,0:T(8,128)(2,1)S(1)} %get-tuple-element.50), channel_id=1, source_target_pairs={{0,40},{1,41},{2,42},{3,43},{4,44},{5,45},{6,46},{7,47},{8,32},{9,... | collective-permute-start | bytes 294920 | tf_op jit(solution)/shard_map/ppermute | solution.py:93
  91.0 2.9 %collective-permute-done.13 = bf16[16,6144]{1,0:T(8,128)(2,1)S(1)} collective-permute-done((bf16[16,6144]{1,0:T(8,128)(2,1)S(1)}, bf16[16,6144]{1,0:T(8,128)(2,1)S(1)}, u32[]{:S(2)}, u32[]{:S(2)}) %collective-permute-start.13) | collective-permute-done | bytes 196640 | tf_op jit(solution)/shard_map/ppermute | solution.py:93
  96.8 3.8 %collective-permute-done.14 = bf16[32,6144]{1,0:T(8,128)(2,1)S(1)} collective-permute-done((bf16[32,6144]{1,0:T(8,128)(2,1)S(1)}, bf16[32,6144]{1,0:T(8,128)(2,1)S(1)}, u32[]{:S(2)}, u32[]{:S(2)}) %collective-permute-start.14) | collective-permute-done | bytes 393248 | tf_op jit(solution)/shard_map/ppermute | solution.py:93
  103.9 2.9 %collective-permute-start.22 = (bf16[64,6144]{1,0:T(8,128)(2,1)S(1)}, bf16[64,6144]{1,0:T(8,128)(2,1)S(1)}, u32[]{:S(2)}, u32[]{:S(2)}) collective-permute-start(bf16[64,6144]{1,0:T(8,128)(2,1)S(1)} %pad_maximum_fusion.3), channel_id=1, source_target_pairs={{0,64},{1,9},{2,66},{3,11},{4,68},{5,13},{6,70},{7,15},{8,72},{9,1... | collective-permute-start | bytes 2359304 | tf_op jit(solution)/shard_map/ppermute | solution.py:93
  106.8 11.7 %collective-permute-start.25 = (bf16[2,256,384]{2,1,0:T(8,128)(2,1)S(1)}, bf16[2,256,384]{2,1,0:T(8,128)(2,1)S(1)}, u32[]{:S(2)}, u32[]{:S(2)}) collective-permute-start(bf16[2,256,384]{2,1,0:T(8,128)(2,1)S(1)} %pad_maximum_fusion.7), channel_id=1, source_target_pairs={{0,1},{1,0},{2,3},{3,2},{4,5},{5,4},{6,7},{7,6},{8,9},{9,8},{10,11... | collective-permute-start | bytes 1179656 | tf_op jit(solution)/shard_map/ppermute | solution.py:31
  120.7 3.2 %collective-permute-start.23 = (bf16[128,6144]{1,0:T(8,128)(2,1)S(1)}, bf16[128,6144]{1,0:T(8,128)(2,1)S(1)}, u32[]{:S(2)}, u32[]{:S(2)}) collective-permute-start(bf16[128,6144]{1,0:T(8,128)(2,1)S(1)} %constant_dynamic-update-slice_fusion.a_ref), channel_id=1, source_target_pairs={{0,64},{1,9},{2,66},{3,11},{4,68},{5,13},{6,70},{7,15},{8,72},{9,1... | collective-permute-start | bytes 4718600 | tf_op jit(solution)/shard_map/ppermute | solution.py:93
  125.7 3.9 %shard_map.90 = f32[2,128,384]{2,1,0:T(8,128)S(1)} custom-call(bf16[128,6144]{1,0:T(8,128)(2,1)S(1)} %constant_dynamic-update-slice_fusion.a_ref, bf16[128,6144]{1,0:T(8,128)(2,1)S(1)} %constant_dynamic-update-slice_fusion.5.h_ref, bf16[384,3072]{1,0:T(8,128)(2,1)S(1)} %copy-done.1, bf16[384,3072]{1,0:T(8,128)(2,1)S(1)} %collective-permute-done.3.there_ref.in2_ref, ...), custom_call_target="tpu_custom_call" | custom-call | flops 1207959552 | bytes 3145728 | tf_op jit(solution)/shard_map/pallas_call | solution.py:163
  130.1 8.7 %collective-permute-start.27 = (bf16[2,128,3072]{2,1,0:T(8,128)(2,1)S(1)}, bf16[2,128,3072]{2,1,0:T(8,128)(2,1)S(1)}, u32[]{:S(2)}, u32[]{:S(2)}) collective-permute-start(bf16[2,128,3072]{2,1,0:T(8,128)(2,1)S(1)} %pad_maximum_fusion.1), channel_id=1, source_target_pairs={{0,1},{1,0},{2,3},{3,2},{4,5},{5,4},{6,7},{7,6},{8,9},{9,8},{10,11... | collective-permute-start | bytes 4718600 | tf_op jit(solution)/shard_map/ppermute | solution.py:31
  138.8 3.2 %collective-permute-done.23.a_ref = bf16[128,6144]{1,0:T(8,128)(2,1)S(1)} collective-permute-done((bf16[128,6144]{1,0:T(8,128)(2,1)S(1)}, bf16[128,6144]{1,0:T(8,128)(2,1)S(1)}, u32[]{:S(2)}, u32[]{:S(2)}) %collective-permute-start.23) | collective-permute-done | bytes 1572896 | tf_op jit(solution)/shard_map/ppermute | solution.py:93
  142.0 2.7 %collective-permute-done.24.h_ref = bf16[128,6144]{1,0:T(8,128)(2,1)S(1)} collective-permute-done((bf16[128,6144]{1,0:T(8,128)(2,1)S(1)}, bf16[128,6144]{1,0:T(8,128)(2,1)S(1)}, u32[]{:S(2)}, u32[]{:S(2)}) %collective-permute-start.24) | collective-permute-done | bytes 1572896 | tf_op jit(solution)/shard_map/ppermute | solution.py:93
  145.0 9.2 %collective-permute-start.26 = (bf16[2,128,3072]{2,1,0:T(8,128)(2,1)S(1)}, bf16[2,128,3072]{2,1,0:T(8,128)(2,1)S(1)}, u32[]{:S(2)}, u32[]{:S(2)}) collective-permute-start(bf16[2,128,3072]{2,1,0:T(8,128)(2,1)S(1)} %pad_maximum_fusion), channel_id=1, source_target_pairs={{0,1},{1,0},{2,3},{3,2},{4,5},{5,4},{6,7},{7,6},{8,9},{9,8},{10,11... | collective-permute-start | bytes 4718600 | tf_op jit(solution)/shard_map/ppermute | solution.py:31
  154.3 3.9 %shard_map.89 = f32[2,128,384]{2,1,0:T(8,128)S(1)} custom-call(bf16[128,6144]{1,0:T(8,128)(2,1)S(1)} %collective-permute-done.23.a_ref, bf16[128,6144]{1,0:T(8,128)(2,1)S(1)} %collective-permute-done.24.h_ref, bf16[384,3072]{1,0:T(8,128)(2,1)S(1)} %copy-done.1, bf16[384,3072]{1,0:T(8,128)(2,1)S(1)} %collective-permute-done.3.there_ref.in2_ref, ...), custom_call_target="tpu_custom_call" | custom-call | flops 1207959552 | bytes 3145728 | tf_op jit(solution)/shard_map/pallas_call | solution.py:163
  158.9 4.2 %collective-permute-start.30 = (bf16[2,64,384]{2,1,0:T(8,128)(2,1)S(1)}, bf16[2,64,384]{2,1,0:T(8,128)(2,1)S(1)}, u32[]{:S(2)}, u32[]{:S(2)}) collective-permute-start(bf16[2,64,384]{2,1,0:T(8,128)(2,1)S(1)} %get-tuple-element.62), channel_id=1, source_target_pairs={{0,6},{1,7},{2,0},{3,1},{4,2},{5,3},{6,4},{7,5},{8,14},{9,15},{10,... | collective-permute-start | bytes 294920 | tf_op jit(solution)/shard_map/ppermute | solution.py:27
  164.6 3.1 %convolution_convert_fusion = bf16[3072,384]{1,0:T(8,128)(2,1)} fusion(bf16[128,3072]{1,0:T(8,128)(2,1)S(1)} %get-tuple-element.40, bf16[128,3072]{1,0:T(8,128)(2,1)S(1)} %get-tuple-element.38, bf16[128,3072]{1,0:T(8,128)(2,1)S(1)} %get-tuple-element.36, bf16[128,3072]{1,0:T(8,128)(2,1)S(1)} %get-tuple-element.34, bf16[256,384]{1,0:T(8,128)(2,1)S(1)} %get-tuple-element.55, ...), kind=kOutput, calls=%fused_computation | convolution fusion | flops 1222508544 | bytes 5898240 | tf_op jit(solution)/shard_map/dot_general | solution.py:243
  (109 shorter events, 53.0 us)
Async XLA Ops:
  0.6 13.4 %collective-permute-start.3 = (bf16[384,3072]{1,0:T(8,128)(2,1)}, bf16[384,3072]{1,0:T(8,128)(2,1)S(1)}, u32[]{:S(2)}, u32[]{:S(2)}) collective-permute-start(bf16[384,3072]{1,0:T(8,128)(2,1)} %in_ref.3), channel_id=1, source_target_pairs={{0,1},{1,0},{2,3},{3,2},{4,5},{5,4},{6,7},{7,6},{8,9},{9,8},{10,11... | collective-permute-start | bytes 7077896 | tf_op jit(solution)/shard_map/ppermute | solution.py:31
  4.0 13.3 %collective-permute-start.5 = (bf16[3072,384]{1,0:T(8,128)(2,1)}, bf16[3072,384]{1,0:T(8,128)(2,1)}, u32[]{:S(2)}, u32[]{:S(2)}) collective-permute-start(bf16[3072,384]{1,0:T(8,128)(2,1)} %out_w_ref.3), channel_id=1, source_target_pairs={{0,1},{1,0},{2,3},{3,2},{4,5},{5,4},{6,7},{7,6},{8,9},{9,8},{10,11... | collective-permute-start | bytes 7077896 | tf_op jit(solution)/shard_map/ppermute | solution.py:31
  5.8 6.8 %collective-permute-start.1 = (bf16[64,768]{1,0:T(8,128)(2,1)S(1)}, bf16[64,768]{1,0:T(8,128)(2,1)S(1)}, u32[]{:S(2)}, u32[]{:S(2)}) collective-permute-start(bf16[64,768]{1,0:T(8,128)(2,1)S(1)} %shard_map.84), channel_id=1, source_target_pairs={{0,4},{1,5},{2,6},{3,7},{4,0},{5,1},{6,2},{7,3},{8,12},{9,13},{10,... | collective-permute-start | bytes 294920 | tf_op jit(solution)/shard_map/ppermute | solution.py:27
  16.2 19.6 %collective-permute-start.4 = (bf16[128,6144]{1,0:T(8,128)(2,1)S(1)}, bf16[128,6144]{1,0:T(8,128)(2,1)S(1)}, u32[]{:S(2)}, u32[]{:S(2)}) collective-permute-start(bf16[128,6144]{1,0:T(8,128)(2,1)S(1)} %shard_map.86), channel_id=1, source_target_pairs={{0,64},{1,9},{2,66},{3,11},{4,68},{5,13},{6,70},{7,15},{8,72},{9,1... | collective-permute-start | bytes 4718600 | tf_op jit(solution)/shard_map/ppermute | solution.py:93
  20.4 22.6 %collective-permute-start.6 = (bf16[128,6144]{1,0:T(8,128)(2,1)S(1)}, bf16[128,6144]{1,0:T(8,128)(2,1)S(1)}, u32[]{:S(2)}, u32[]{:S(2)}) collective-permute-start(bf16[128,6144]{1,0:T(8,128)(2,1)S(1)} %shard_map.87), channel_id=1, source_target_pairs={{0,192},{1,57},{2,194},{3,59},{4,196},{5,61},{6,198},{7,63},{8,200... | collective-permute-start | bytes 4718600 | tf_op jit(solution)/shard_map/ppermute | solution.py:93
  43.3 12.7 %collective-permute-start.7 = (bf16[64,6144]{1,0:T(8,128)(2,1)S(1)}, bf16[64,6144]{1,0:T(8,128)(2,1)S(1)}, u32[]{:S(2)}, u32[]{:S(2)}) collective-permute-start(bf16[64,6144]{1,0:T(8,128)(2,1)S(1)} %get-tuple-element.28), channel_id=1, source_target_pairs={{0,192},{1,57},{2,194},{3,59},{4,196},{5,61},{6,198},{7,63},{8,200... | collective-permute-start | bytes 2359304 | tf_op jit(solution)/shard_map/ppermute | solution.py:93
  46.7 11.1 %collective-permute-start.8 = (bf16[64,6144]{1,0:T(8,128)(2,1)S(1)}, bf16[64,6144]{1,0:T(8,128)(2,1)S(1)}, u32[]{:S(2)}, u32[]{:S(2)}) collective-permute-start(bf16[64,6144]{1,0:T(8,128)(2,1)S(1)} %get-tuple-element.27), channel_id=1, source_target_pairs={{0,64},{1,9},{2,66},{3,11},{4,68},{5,13},{6,70},{7,15},{8,72},{9,1... | collective-permute-start | bytes 2359304 | tf_op jit(solution)/shard_map/ppermute | solution.py:93
  57.9 8.4 %collective-permute-start.16 = (bf16[32,6144]{1,0:T(8,128)(2,1)S(1)}, bf16[32,6144]{1,0:T(8,128)(2,1)S(1)}, u32[]{:S(2)}, u32[]{:S(2)}) collective-permute-start(bf16[32,6144]{1,0:T(8,128)(2,1)S(1)} %get-tuple-element.30), channel_id=1, source_target_pairs={{0,56},{1,193},{2,58},{3,195},{4,60},{5,197},{6,62},{7,199},{8,16}... | collective-permute-start | bytes 1179656 | tf_op jit(solution)/shard_map/ppermute | solution.py:93
  60.7 7.0 %collective-permute-start.9 = (bf16[32,6144]{1,0:T(8,128)(2,1)S(1)}, bf16[32,6144]{1,0:T(8,128)(2,1)S(1)}, u32[]{:S(2)}, u32[]{:S(2)}) collective-permute-start(bf16[32,6144]{1,0:T(8,128)(2,1)S(1)} %get-tuple-element.32), channel_id=1, source_target_pairs={{0,8},{1,65},{2,10},{3,67},{4,12},{5,69},{6,14},{7,71},{8,0},{9,73... | collective-permute-start | bytes 1179656 | tf_op jit(solution)/shard_map/ppermute | solution.py:93
  71.3 9.5 %collective-permute-start.18 = (bf16[8,6144]{1,0:T(8,128)(2,1)S(1)}, bf16[8,6144]{1,0:T(8,128)(2,1)S(1)}, u32[]{:S(2)}, u32[]{:S(2)}) collective-permute-start(bf16[8,6144]{1,0:T(8,128)(2,1)S(1)} %fusion.33), channel_id=1, source_target_pairs={{0,40},{1,41},{2,42},{3,43},{4,44},{5,45},{6,46},{7,47},{8,32},{9,... | collective-permute-start | bytes 294920 | tf_op jit(solution)/shard_map/ppermute | solution.py:93
  73.6 7.2 %collective-permute-start.11 = (bf16[8,6144]{1,0:T(8,128)(2,1)S(1)}, bf16[8,6144]{1,0:T(8,128)(2,1)S(1)}, u32[]{:S(2)}, u32[]{:S(2)}) collective-permute-start(bf16[8,6144]{1,0:T(8,128)(2,1)S(1)} %fusion.35), channel_id=1, source_target_pairs={{0,24},{1,25},{2,26},{3,27},{4,28},{5,29},{6,30},{7,31},{8,48},{9,... | collective-permute-start | bytes 294920 | tf_op jit(solution)/shard_map/ppermute | solution.py:93
  82.8 8.1 %collective-permute-start.19 = (bf16[8,6144]{1,0:T(8,128)(2,1)S(1)}, bf16[8,6144]{1,0:T(8,128)(2,1)S(1)}, u32[]{:S(2)}, u32[]{:S(2)}) collective-permute-start(bf16[8,6144]{1,0:T(8,128)(2,1)S(1)} %get-tuple-element.50), channel_id=1, source_target_pairs={{0,40},{1,41},{2,42},{3,43},{4,44},{5,45},{6,46},{7,47},{8,32},{9,... | collective-permute-start | bytes 294920 | tf_op jit(solution)/shard_map/ppermute | solution.py:93
  93.9 6.7 %collective-permute-start.14 = (bf16[32,6144]{1,0:T(8,128)(2,1)S(1)}, bf16[32,6144]{1,0:T(8,128)(2,1)S(1)}, u32[]{:S(2)}, u32[]{:S(2)}) collective-permute-start(bf16[32,6144]{1,0:T(8,128)(2,1)S(1)} %pad_maximum_fusion.5), channel_id=1, source_target_pairs={{0,8},{1,65},{2,10},{3,67},{4,12},{5,69},{6,14},{7,71},{8,0},{9,73... | collective-permute-start | bytes 1179656 | tf_op jit(solution)/shard_map/ppermute | solution.py:93
  95.6 8.2 %collective-permute-start.21 = (bf16[32,6144]{1,0:T(8,128)(2,1)S(1)}, bf16[32,6144]{1,0:T(8,128)(2,1)S(1)}, u32[]{:S(2)}, u32[]{:S(2)}) collective-permute-start(bf16[32,6144]{1,0:T(8,128)(2,1)S(1)} %pad_maximum_fusion.6), channel_id=1, source_target_pairs={{0,56},{1,193},{2,58},{3,195},{4,60},{5,197},{6,62},{7,199},{8,16}... | collective-permute-start | bytes 1179656 | tf_op jit(solution)/shard_map/ppermute | solution.py:93
  100.7 19.2 %collective-permute-start.15 = (bf16[64,6144]{1,0:T(8,128)(2,1)S(1)}, bf16[64,6144]{1,0:T(8,128)(2,1)S(1)}, u32[]{:S(2)}, u32[]{:S(2)}) collective-permute-start(bf16[64,6144]{1,0:T(8,128)(2,1)S(1)} %pad_maximum_fusion.2), channel_id=1, source_target_pairs={{0,192},{1,57},{2,194},{3,59},{4,196},{5,61},{6,198},{7,63},{8,200... | collective-permute-start | bytes 2359304 | tf_op jit(solution)/shard_map/ppermute | solution.py:93
  103.9 16.5 %collective-permute-start.22 = (bf16[64,6144]{1,0:T(8,128)(2,1)S(1)}, bf16[64,6144]{1,0:T(8,128)(2,1)S(1)}, u32[]{:S(2)}, u32[]{:S(2)}) collective-permute-start(bf16[64,6144]{1,0:T(8,128)(2,1)S(1)} %pad_maximum_fusion.3), channel_id=1, source_target_pairs={{0,64},{1,9},{2,66},{3,11},{4,68},{5,13},{6,70},{7,15},{8,72},{9,1... | collective-permute-start | bytes 2359304 | tf_op jit(solution)/shard_map/ppermute | solution.py:93
  106.8 13.1 %collective-permute-start.25 = (bf16[2,256,384]{2,1,0:T(8,128)(2,1)S(1)}, bf16[2,256,384]{2,1,0:T(8,128)(2,1)S(1)}, u32[]{:S(2)}, u32[]{:S(2)}) collective-permute-start(bf16[2,256,384]{2,1,0:T(8,128)(2,1)S(1)} %pad_maximum_fusion.7), channel_id=1, source_target_pairs={{0,1},{1,0},{2,3},{3,2},{4,5},{5,4},{6,7},{7,6},{8,9},{9,8},{10,11... | collective-permute-start | bytes 1179656 | tf_op jit(solution)/shard_map/ppermute | solution.py:31
  120.7 21.3 %collective-permute-start.23 = (bf16[128,6144]{1,0:T(8,128)(2,1)S(1)}, bf16[128,6144]{1,0:T(8,128)(2,1)S(1)}, u32[]{:S(2)}, u32[]{:S(2)}) collective-permute-start(bf16[128,6144]{1,0:T(8,128)(2,1)S(1)} %constant_dynamic-update-slice_fusion.a_ref), channel_id=1, source_target_pairs={{0,64},{1,9},{2,66},{3,11},{4,68},{5,13},{6,70},{7,15},{8,72},{9,1... | collective-permute-start | bytes 4718600 | tf_op jit(solution)/shard_map/ppermute | solution.py:93
  123.8 20.8 %collective-permute-start.24 = (bf16[128,6144]{1,0:T(8,128)(2,1)S(1)}, bf16[128,6144]{1,0:T(8,128)(2,1)S(1)}, u32[]{:S(2)}, u32[]{:S(2)}) collective-permute-start(bf16[128,6144]{1,0:T(8,128)(2,1)S(1)} %constant_dynamic-update-slice_fusion.5.h_ref), channel_id=1, source_target_pairs={{0,192},{1,57},{2,194},{3,59},{4,196},{5,61},{6,198},{7,63},{8,200... | collective-permute-start | bytes 4718600 | tf_op jit(solution)/shard_map/ppermute | solution.py:93
  130.1 34.3 %collective-permute-start.27 = (bf16[2,128,3072]{2,1,0:T(8,128)(2,1)S(1)}, bf16[2,128,3072]{2,1,0:T(8,128)(2,1)S(1)}, u32[]{:S(2)}, u32[]{:S(2)}) collective-permute-start(bf16[2,128,3072]{2,1,0:T(8,128)(2,1)S(1)} %pad_maximum_fusion.1), channel_id=1, source_target_pairs={{0,1},{1,0},{2,3},{3,2},{4,5},{5,4},{6,7},{7,6},{8,9},{9,8},{10,11... | collective-permute-start | bytes 4718600 | tf_op jit(solution)/shard_map/ppermute | solution.py:31
  145.0 19.5 %collective-permute-start.26 = (bf16[2,128,3072]{2,1,0:T(8,128)(2,1)S(1)}, bf16[2,128,3072]{2,1,0:T(8,128)(2,1)S(1)}, u32[]{:S(2)}, u32[]{:S(2)}) collective-permute-start(bf16[2,128,3072]{2,1,0:T(8,128)(2,1)S(1)} %pad_maximum_fusion), channel_id=1, source_target_pairs={{0,1},{1,0},{2,3},{3,2},{4,5},{5,4},{6,7},{7,6},{8,9},{9,8},{10,11... | collective-permute-start | bytes 4718600 | tf_op jit(solution)/shard_map/ppermute | solution.py:31
  158.9 11.4 %collective-permute-start.30 = (bf16[2,64,384]{2,1,0:T(8,128)(2,1)S(1)}, bf16[2,64,384]{2,1,0:T(8,128)(2,1)S(1)}, u32[]{:S(2)}, u32[]{:S(2)}) collective-permute-start(bf16[2,64,384]{2,1,0:T(8,128)(2,1)S(1)} %get-tuple-element.62), channel_id=1, source_target_pairs={{0,6},{1,7},{2,0},{3,1},{4,2},{5,3},{6,4},{7,5},{8,14},{9,15},{10,... | collective-permute-start | bytes 294920 | tf_op jit(solution)/shard_map/ppermute | solution.py:27
  163.1 7.3 %collective-permute-start.29 = (bf16[2,64,384]{2,1,0:T(8,128)(2,1)S(1)}, bf16[2,64,384]{2,1,0:T(8,128)(2,1)S(1)}, u32[]{:S(2)}, u32[]{:S(2)}) collective-permute-start(bf16[2,64,384]{2,1,0:T(8,128)(2,1)S(1)} %get-tuple-element.63), channel_id=1, source_target_pairs={{0,4},{1,5},{2,6},{3,7},{4,0},{5,1},{6,2},{7,3},{8,12},{9,13},{10,... | collective-permute-start | bytes 294920 | tf_op jit(solution)/shard_map/ppermute | solution.py:27
  163.6 7.8 %collective-permute-start.28 = (bf16[2,64,384]{2,1,0:T(8,128)(2,1)S(1)}, bf16[2,64,384]{2,1,0:T(8,128)(2,1)S(1)}, u32[]{:S(2)}, u32[]{:S(2)}) collective-permute-start(bf16[2,64,384]{2,1,0:T(8,128)(2,1)S(1)} %get-tuple-element.61), channel_id=1, source_target_pairs={{0,2},{1,3},{2,4},{3,5},{4,6},{5,7},{6,0},{7,1},{8,10},{9,11},{10,... | collective-permute-start | bytes 294920 | tf_op jit(solution)/shard_map/ppermute | solution.py:27
  (11 other events, 44.6 us)

commit v2 on v1

--- a/solution.py
+++ b/solution.py
@@ -194,7 +194,7 @@
 
     for step in range(5):
         got = [exchange(send[a], step, a) for a in both]
-        if step < 2:
+        if step < 1:
             got = together(got)
         left = keep[0].shape[0] // 2
         if step == 4:

time: 172 us -> 169 us (0.983)
  waiting for transfers between devices: 65.4 us -> 55.7 us
  starting transfers between devices: 74.9 us -> 80.9 us
    ppermute x20, waiting for transfers between devices: 59.8 us -> 50 us  [exchange(): return lax.ppermute(x, ('depth', 'row', 'col'), pairs)]
    ppermute x20, starting transfers between devices: 33 us -> 39.9 us  [exchange(): return lax.ppermute(x, ('depth', 'row', 'col'), pairs)]
    ppermute x6, starting transfers between devices: 8.77 us -> 5.43 us  [shift_y(): return lax.ppermute(x, 'col', [(i, (i + 2 * k) % 8) for i in range(8)])]
    ppermute x5, starting transfers between devices: 33.1 us -> 35.6 us  [swap_core(): return lax.ppermute(x, 'col', [(i, i ^ 1) for i in range(8)])]
  transfers between devices with their start and end apart: 31 -> 31, of which waited for: 23 -> 20; matrix products, arithmetic and copies ran while one was open for 6% -> 6% of each run, Pallas kernels for 9% -> 10%
where the time goes in v2:
time: 169 us; the launch traced here: 168 us
  starting transfers between devices  80.9 us (48%)
  waiting for transfers between devices  55.7 us (33%)
  Pallas kernels  16.1 us (10%)
  matrix products  6.86 us (4%)
  local copies, waits for them, and re-layouts  4.82 us (3%)
  other arithmetic  2.89 us (2%)
    ppermute x20, waiting for transfers between devices, exchange(): return lax.ppermute(x, ('depth', 'row', 'col'), pairs)  50 us
    ppermute x20, starting transfers between devices, exchange(): return lax.ppermute(x, ('depth', 'row', 'col'), pairs)  39.9 us
    ppermute x5, starting transfers between devices, swap_core(): return lax.ppermute(x, 'col', [(i, i ^ 1) for i in range(8)])  35.6 us
    pallas_call x4, Pallas kernels, partials(): pl.pallas_call(body, in_specs=[VMEM] * 3, out_specs=VMEM, out_shape=jax.S...  8.28 us
    pallas_call x2, Pallas kernels, products(): pl.pallas_call(body, in_specs=[VMEM] * 6, out_specs=VMEM, out_shape=jax.S...  7.86 us
    dot_general x2, matrix products, over_tokens(): lax.dot_general(x, y, (((0,), (0,)), ((), ())), preferred_element_type=F32)  5.72 us
    ppermute x6, starting transfers between devices, shift_y(): return lax.ppermute(x, 'col', [(i, (i + 2 * k) % 8) for i in range(8)])  5.43 us
    ppermute x6, waiting for transfers between devices, shift_y(): return lax.ppermute(x, 'col', [(i, (i + 2 * k) % 8) for i in range(8)])  4.24 us
  transfers between devices with their start and end apart: 31, of which 20 were waited for; matrix products, arithmetic and copies ran while one was open for 6% of the time, Pallas kernels for 10%

profile of v2, /device:TPU:1, one launch (start us, length us, event | category | flops | bytes accessed | tf_op | source)
XLA Modules:
  0.0 168.3 jit_solution(17229946083801477416)
XLA Ops:
  0.6 3.3 %collective-permute-start.3 = (bf16[384,3072]{1,0:T(8,128)(2,1)}, bf16[384,3072]{1,0:T(8,128)(2,1)S(1)}, u32[]{:S(2)}, u32[]{:S(2)}) collective-permute-start(bf16[384,3072]{1,0:T(8,128)(2,1)} %in_ref.3), channel_id=1, source_target_pairs={{0,1},{1,0},{2,3},{3,2},{4,5},{5,4},{6,7},{7,6},{8,9},{9,8},{10,11... | collective-permute-start | bytes 7077896 | tf_op jit(solution)/shard_map/ppermute | solution.py:31
  17.2 3.1 %shard_map.87 = bf16[128,6144]{1,0:T(8,128)(2,1)S(1)} custom-call(bf16[256,384]{1,0:T(8,128)(2,1)S(1)} %get-tuple-element.55.tok_ref, bf16[3072,384]{1,0:T(8,128)(2,1)S(1)} %copy-done, bf16[3072,384]{1,0:T(8,128)(2,1)} %collective-permute-done.5.there_ref.out2_ref), custom_call_target="tpu_custom_call" | custom-call | flops 603979776 | bytes 1572864 | tf_op jit(solution)/shard_map/pallas_call | solution.py:137
  20.4 4.8 %collective-permute-start.6 = (bf16[128,6144]{1,0:T(8,128)(2,1)S(1)}, bf16[128,6144]{1,0:T(8,128)(2,1)S(1)}, u32[]{:S(2)}, u32[]{:S(2)}) collective-permute-start(bf16[128,6144]{1,0:T(8,128)(2,1)S(1)} %shard_map.87), channel_id=1, source_target_pairs={{0,192},{1,57},{2,194},{3,59},{4,196},{5,61},{6,198},{7,63},{8,200... | collective-permute-start | bytes 4718600 | tf_op jit(solution)/shard_map/ppermute | solution.py:93
  25.1 3.1 %shard_map.88 = bf16[128,6144]{1,0:T(8,128)(2,1)S(1)} custom-call(bf16[256,384]{1,0:T(8,128)(2,1)S(1)} %get-tuple-element.55.tok_ref, bf16[3072,384]{1,0:T(8,128)(2,1)S(1)} %copy-done, bf16[3072,384]{1,0:T(8,128)(2,1)} %collective-permute-done.5.there_ref.out2_ref), custom_call_target="tpu_custom_call" | custom-call | flops 603979776 | bytes 1572864 | tf_op jit(solution)/shard_map/pallas_call | solution.py:137
  29.3 6.6 %collective-permute-done.4 = bf16[128,6144]{1,0:T(8,128)(2,1)S(1)} collective-permute-done((bf16[128,6144]{1,0:T(8,128)(2,1)S(1)}, bf16[128,6144]{1,0:T(8,128)(2,1)S(1)}, u32[]{:S(2)}, u32[]{:S(2)}) %collective-permute-start.4) | collective-permute-done | bytes 1572896 | tf_op jit(solution)/shard_map/ppermute | solution.py:93
  35.9 7.0 %collective-permute-done.6 = bf16[128,6144]{1,0:T(8,128)(2,1)S(1)} collective-permute-done((bf16[128,6144]{1,0:T(8,128)(2,1)S(1)}, bf16[128,6144]{1,0:T(8,128)(2,1)S(1)}, u32[]{:S(2)}, u32[]{:S(2)}) %collective-permute-start.6) | collective-permute-done | bytes 1572896 | tf_op jit(solution)/shard_map/ppermute | solution.py:93
  43.7 3.0 %collective-permute-start.7 = (bf16[64,6144]{1,0:T(8,128)(2,1)S(1)}, bf16[64,6144]{1,0:T(8,128)(2,1)S(1)}, u32[]{:S(2)}, u32[]{:S(2)}) collective-permute-start(bf16[64,6144]{1,0:T(8,128)(2,1)S(1)} %get-tuple-element.24), channel_id=1, source_target_pairs={{0,192},{1,57},{2,194},{3,59},{4,196},{5,61},{6,198},{7,63},{8,200... | collective-permute-start | bytes 2359304 | tf_op jit(solution)/shard_map/ppermute | solution.py:93
  46.8 7.7 %collective-permute-done.15 = bf16[64,6144]{1,0:T(8,128)(2,1)S(1)} collective-permute-done((bf16[64,6144]{1,0:T(8,128)(2,1)S(1)}, bf16[64,6144]{1,0:T(8,128)(2,1)S(1)}, u32[]{:S(2)}, u32[]{:S(2)}) %collective-permute-start.15) | collective-permute-done | bytes 786464 | tf_op jit(solution)/shard_map/ppermute | solution.py:93
  54.6 2.8 %collective-permute-start.16 = (bf16[32,6144]{1,0:T(8,128)(2,1)S(1)}, bf16[32,6144]{1,0:T(8,128)(2,1)S(1)}, u32[]{:S(2)}, u32[]{:S(2)}) collective-permute-start(bf16[32,6144]{1,0:T(8,128)(2,1)S(1)} %get-tuple-element.26), channel_id=1, source_target_pairs={{0,56},{1,193},{2,58},{3,195},{4,60},{5,197},{6,62},{7,199},{8,16}... | collective-permute-start | bytes 1179656 | tf_op jit(solution)/shard_map/ppermute | solution.py:93
  57.7 5.4 %collective-permute-done.16 = bf16[32,6144]{1,0:T(8,128)(2,1)S(1)} collective-permute-done((bf16[32,6144]{1,0:T(8,128)(2,1)S(1)}, bf16[32,6144]{1,0:T(8,128)(2,1)S(1)}, u32[]{:S(2)}, u32[]{:S(2)}) %collective-permute-start.16) | collective-permute-done | bytes 393248 | tf_op jit(solution)/shard_map/ppermute | solution.py:93
  68.1 4.3 %collective-permute-start.18 = (bf16[8,6144]{1,0:T(8,128)(2,1)S(1)}, bf16[8,6144]{1,0:T(8,128)(2,1)S(1)}, u32[]{:S(2)}, u32[]{:S(2)}) collective-permute-start(bf16[8,6144]{1,0:T(8,128)(2,1)S(1)} %fusion.33), channel_id=1, source_target_pairs={{0,40},{1,41},{2,42},{3,43},{4,44},{5,45},{6,46},{7,47},{8,32},{9,... | collective-permute-start | bytes 294920 | tf_op jit(solution)/shard_map/ppermute | solution.py:93
  75.2 2.6 %collective-permute-done.10 = bf16[8,6144]{1,0:T(8,128)(2,1)S(1)} collective-permute-done((bf16[8,6144]{1,0:T(8,128)(2,1)S(1)}, bf16[8,6144]{1,0:T(8,128)(2,1)S(1)}, u32[]{:S(2)}, u32[]{:S(2)}) %collective-permute-start.10) | collective-permute-done | bytes 98336 | tf_op jit(solution)/shard_map/ppermute | solution.py:93
  79.7 5.4 %collective-permute-start.19 = (bf16[8,6144]{1,0:T(8,128)(2,1)S(1)}, bf16[8,6144]{1,0:T(8,128)(2,1)S(1)}, u32[]{:S(2)}, u32[]{:S(2)}) collective-permute-start(bf16[8,6144]{1,0:T(8,128)(2,1)S(1)} %get-tuple-element.46), channel_id=1, source_target_pairs={{0,40},{1,41},{2,42},{3,43},{4,44},{5,45},{6,46},{7,47},{8,32},{9,... | collective-permute-start | bytes 294920 | tf_op jit(solution)/shard_map/ppermute | solution.py:93
  95.0 2.9 %collective-permute-done.13 = bf16[32,6144]{1,0:T(8,128)(2,1)S(1)} collective-permute-done((bf16[32,6144]{1,0:T(8,128)(2,1)S(1)}, bf16[32,6144]{1,0:T(8,128)(2,1)S(1)}, u32[]{:S(2)}, u32[]{:S(2)}) %collective-permute-start.13) | collective-permute-done | bytes 393248 | tf_op jit(solution)/shard_map/ppermute | solution.py:93
  101.2 4.7 %collective-permute-start.22 = (bf16[64,6144]{1,0:T(8,128)(2,1)S(1)}, bf16[64,6144]{1,0:T(8,128)(2,1)S(1)}, u32[]{:S(2)}, u32[]{:S(2)}) collective-permute-start(bf16[64,6144]{1,0:T(8,128)(2,1)S(1)} %pad_maximum_fusion.3), channel_id=1, source_target_pairs={{0,64},{1,9},{2,66},{3,11},{4,68},{5,13},{6,70},{7,15},{8,72},{9,1... | collective-permute-start | bytes 2359304 | tf_op jit(solution)/shard_map/ppermute | solution.py:93
  105.9 13.2 %collective-permute-start.25 = (bf16[2,256,384]{2,1,0:T(8,128)(2,1)S(1)}, bf16[2,256,384]{2,1,0:T(8,128)(2,1)S(1)}, u32[]{:S(2)}, u32[]{:S(2)}) collective-permute-start(bf16[2,256,384]{2,1,0:T(8,128)(2,1)S(1)} %pad_maximum_fusion.7), channel_id=1, source_target_pairs={{0,1},{1,0},{2,3},{3,2},{4,5},{5,4},{6,7},{7,6},{8,9},{9,8},{10,11... | collective-permute-start | bytes 1179656 | tf_op jit(solution)/shard_map/ppermute | solution.py:31
  123.9 3.9 %shard_map.90 = f32[2,128,384]{2,1,0:T(8,128)S(1)} custom-call(bf16[128,6144]{1,0:T(8,128)(2,1)S(1)} %constant_dynamic-update-slice_fusion.a_ref, bf16[128,6144]{1,0:T(8,128)(2,1)S(1)} %constant_dynamic-update-slice_fusion.5.h_ref, bf16[384,3072]{1,0:T(8,128)(2,1)S(1)} %copy-done.1, bf16[384,3072]{1,0:T(8,128)(2,1)S(1)} %collective-permute-done.3.there_ref.in2_ref, ...), custom_call_target="tpu_custom_call" | custom-call | flops 1207959552 | bytes 3145728 | tf_op jit(solution)/shard_map/pallas_call | solution.py:163
  128.3 9.0 %collective-permute-start.27 = (bf16[2,128,3072]{2,1,0:T(8,128)(2,1)S(1)}, bf16[2,128,3072]{2,1,0:T(8,128)(2,1)S(1)}, u32[]{:S(2)}, u32[]{:S(2)}) collective-permute-start(bf16[2,128,3072]{2,1,0:T(8,128)(2,1)S(1)} %pad_maximum_fusion.1), channel_id=1, source_target_pairs={{0,1},{1,0},{2,3},{3,2},{4,5},{5,4},{6,7},{7,6},{8,9},{9,8},{10,11... | collective-permute-start | bytes 4718600 | tf_op jit(solution)/shard_map/ppermute | solution.py:31
  137.2 3.6 %collective-permute-done.23.a_ref = bf16[128,6144]{1,0:T(8,128)(2,1)S(1)} collective-permute-done((bf16[128,6144]{1,0:T(8,128)(2,1)S(1)}, bf16[128,6144]{1,0:T(8,128)(2,1)S(1)}, u32[]{:S(2)}, u32[]{:S(2)}) %collective-permute-start.23) | collective-permute-done | bytes 1572896 | tf_op jit(solution)/shard_map/ppermute | solution.py:93
  140.8 2.7 %collective-permute-done.24.h_ref = bf16[128,6144]{1,0:T(8,128)(2,1)S(1)} collective-permute-done((bf16[128,6144]{1,0:T(8,128)(2,1)S(1)}, bf16[128,6144]{1,0:T(8,128)(2,1)S(1)}, u32[]{:S(2)}, u32[]{:S(2)}) %collective-permute-start.24) | collective-permute-done | bytes 1572896 | tf_op jit(solution)/shard_map/ppermute | solution.py:93
  143.9 9.9 %collective-permute-start.26 = (bf16[2,128,3072]{2,1,0:T(8,128)(2,1)S(1)}, bf16[2,128,3072]{2,1,0:T(8,128)(2,1)S(1)}, u32[]{:S(2)}, u32[]{:S(2)}) collective-permute-start(bf16[2,128,3072]{2,1,0:T(8,128)(2,1)S(1)} %pad_maximum_fusion), channel_id=1, source_target_pairs={{0,1},{1,0},{2,3},{3,2},{4,5},{5,4},{6,7},{7,6},{8,9},{9,8},{10,11... | collective-permute-start | bytes 4718600 | tf_op jit(solution)/shard_map/ppermute | solution.py:31
  153.9 3.9 %shard_map.89 = f32[2,128,384]{2,1,0:T(8,128)S(1)} custom-call(bf16[128,6144]{1,0:T(8,128)(2,1)S(1)} %collective-permute-done.23.a_ref, bf16[128,6144]{1,0:T(8,128)(2,1)S(1)} %collective-permute-done.24.h_ref, bf16[384,3072]{1,0:T(8,128)(2,1)S(1)} %copy-done.1, bf16[384,3072]{1,0:T(8,128)(2,1)S(1)} %collective-permute-done.3.there_ref.in2_ref, ...), custom_call_target="tpu_custom_call" | custom-call | flops 1207959552 | bytes 3145728 | tf_op jit(solution)/shard_map/pallas_call | solution.py:163
  160.8 3.1 %convolution_convert_fusion = bf16[3072,384]{1,0:T(8,128)(2,1)} fusion(bf16[128,3072]{1,0:T(8,128)(2,1)S(1)} %get-tuple-element.36, bf16[128,3072]{1,0:T(8,128)(2,1)S(1)} %get-tuple-element.34, bf16[128,3072]{1,0:T(8,128)(2,1)S(1)} %get-tuple-element.32, bf16[128,3072]{1,0:T(8,128)(2,1)S(1)} %get-tuple-element.30, bf16[256,384]{1,0:T(8,128)(2,1)S(1)} %get-tuple-element.51, ...), kind=kOutput, calls=%fused_computation | convolution fusion | flops 1222508544 | bytes 5898240 | tf_op jit(solution)/shard_map/dot_general | solution.py:243
  163.9 2.6 %convolution_convert_fusion.1 = bf16[384,3072]{1,0:T(8,128)(2,1)} fusion(bf16[128,3072]{1,0:T(8,128)(2,1)S(1)} %get-tuple-element.37, bf16[128,3072]{1,0:T(8,128)(2,1)S(1)} %get-tuple-element.35, bf16[128,3072]{1,0:T(8,128)(2,1)S(1)} %get-tuple-element.40, bf16[128,3072]{1,0:T(8,128)(2,1)S(1)} %get-tuple-element.38, ...), kind=kOutput, calls=%fused_computation.1 | convolution fusion | flops 1222508544 | bytes 5898240 | tf_op jit(solution)/shard_map/dot_general | solution.py:243
  (109 shorter events, 48.4 us)
Async XLA Ops:
  0.6 13.4 %collective-permute-start.3 = (bf16[384,3072]{1,0:T(8,128)(2,1)}, bf16[384,3072]{1,0:T(8,128)(2,1)S(1)}, u32[]{:S(2)}, u32[]{:S(2)}) collective-permute-start(bf16[384,3072]{1,0:T(8,128)(2,1)} %in_ref.3), channel_id=1, source_target_pairs={{0,1},{1,0},{2,3},{3,2},{4,5},{5,4},{6,7},{7,6},{8,9},{9,8},{10,11... | collective-permute-start | bytes 7077896 | tf_op jit(solution)/shard_map/ppermute | solution.py:31
  4.0 13.3 %collective-permute-start.5 = (bf16[3072,384]{1,0:T(8,128)(2,1)}, bf16[3072,384]{1,0:T(8,128)(2,1)}, u32[]{:S(2)}, u32[]{:S(2)}) collective-permute-start(bf16[3072,384]{1,0:T(8,128)(2,1)} %out_w_ref.3), channel_id=1, source_target_pairs={{0,1},{1,0},{2,3},{3,2},{4,5},{5,4},{6,7},{7,6},{8,9},{9,8},{10,11... | collective-permute-start | bytes 7077896 | tf_op jit(solution)/shard_map/ppermute | solution.py:31
  5.8 6.8 %collective-permute-start.1 = (bf16[64,768]{1,0:T(8,128)(2,1)S(1)}, bf16[64,768]{1,0:T(8,128)(2,1)S(1)}, u32[]{:S(2)}, u32[]{:S(2)}) collective-permute-start(bf16[64,768]{1,0:T(8,128)(2,1)S(1)} %shard_map.84), channel_id=1, source_target_pairs={{0,4},{1,5},{2,6},{3,7},{4,0},{5,1},{6,2},{7,3},{8,12},{9,13},{10,... | collective-permute-start | bytes 294920 | tf_op jit(solution)/shard_map/ppermute | solution.py:27
  16.3 19.6 %collective-permute-start.4 = (bf16[128,6144]{1,0:T(8,128)(2,1)S(1)}, bf16[128,6144]{1,0:T(8,128)(2,1)S(1)}, u32[]{:S(2)}, u32[]{:S(2)}) collective-permute-start(bf16[128,6144]{1,0:T(8,128)(2,1)S(1)} %shard_map.86), channel_id=1, source_target_pairs={{0,64},{1,9},{2,66},{3,11},{4,68},{5,13},{6,70},{7,15},{8,72},{9,1... | collective-permute-start | bytes 4718600 | tf_op jit(solution)/shard_map/ppermute | solution.py:93
  20.4 22.6 %collective-permute-start.6 = (bf16[128,6144]{1,0:T(8,128)(2,1)S(1)}, bf16[128,6144]{1,0:T(8,128)(2,1)S(1)}, u32[]{:S(2)}, u32[]{:S(2)}) collective-permute-start(bf16[128,6144]{1,0:T(8,128)(2,1)S(1)} %shard_map.87), channel_id=1, source_target_pairs={{0,192},{1,57},{2,194},{3,59},{4,196},{5,61},{6,198},{7,63},{8,200... | collective-permute-start | bytes 4718600 | tf_op jit(solution)/shard_map/ppermute | solution.py:93
  43.3 11.2 %collective-permute-start.15 = (bf16[64,6144]{1,0:T(8,128)(2,1)S(1)}, bf16[64,6144]{1,0:T(8,128)(2,1)S(1)}, u32[]{:S(2)}, u32[]{:S(2)}) collective-permute-start(bf16[64,6144]{1,0:T(8,128)(2,1)S(1)} %get-tuple-element.22), channel_id=1, source_target_pairs={{0,64},{1,9},{2,66},{3,11},{4,68},{5,13},{6,70},{7,15},{8,72},{9,1... | collective-permute-start | bytes 2359304 | tf_op jit(solution)/shard_map/ppermute | solution.py:93
  43.7 13.7 %collective-permute-start.7 = (bf16[64,6144]{1,0:T(8,128)(2,1)S(1)}, bf16[64,6144]{1,0:T(8,128)(2,1)S(1)}, u32[]{:S(2)}, u32[]{:S(2)}) collective-permute-start(bf16[64,6144]{1,0:T(8,128)(2,1)S(1)} %get-tuple-element.24), channel_id=1, source_target_pairs={{0,192},{1,57},{2,194},{3,59},{4,196},{5,61},{6,198},{7,63},{8,200... | collective-permute-start | bytes 2359304 | tf_op jit(solution)/shard_map/ppermute | solution.py:93
  54.6 8.4 %collective-permute-start.16 = (bf16[32,6144]{1,0:T(8,128)(2,1)S(1)}, bf16[32,6144]{1,0:T(8,128)(2,1)S(1)}, u32[]{:S(2)}, u32[]{:S(2)}) collective-permute-start(bf16[32,6144]{1,0:T(8,128)(2,1)S(1)} %get-tuple-element.26), channel_id=1, source_target_pairs={{0,56},{1,193},{2,58},{3,195},{4,60},{5,197},{6,62},{7,199},{8,16}... | collective-permute-start | bytes 1179656 | tf_op jit(solution)/shard_map/ppermute | solution.py:93
  57.6 7.0 %collective-permute-start.8 = (bf16[32,6144]{1,0:T(8,128)(2,1)S(1)}, bf16[32,6144]{1,0:T(8,128)(2,1)S(1)}, u32[]{:S(2)}, u32[]{:S(2)}) collective-permute-start(bf16[32,6144]{1,0:T(8,128)(2,1)S(1)} %get-tuple-element.28), channel_id=1, source_target_pairs={{0,8},{1,65},{2,10},{3,67},{4,12},{5,69},{6,14},{7,71},{8,0},{9,73... | collective-permute-start | bytes 1179656 | tf_op jit(solution)/shard_map/ppermute | solution.py:93
  64.7 7.7 %collective-permute-start.9 = (bf16[16,6144]{1,0:T(8,128)(2,1)S(1)}, bf16[16,6144]{1,0:T(8,128)(2,1)S(1)}, u32[]{:S(2)}, u32[]{:S(2)}) collective-permute-start(bf16[16,6144]{1,0:T(8,128)(2,1)S(1)} %get-tuple-element.44), channel_id=1, source_target_pairs={{0,56},{1,193},{2,58},{3,195},{4,60},{5,197},{6,62},{7,199},{8,16}... | collective-permute-start | bytes 589832 | tf_op jit(solution)/shard_map/ppermute | solution.py:93
  68.1 7.1 %collective-permute-start.18 = (bf16[8,6144]{1,0:T(8,128)(2,1)S(1)}, bf16[8,6144]{1,0:T(8,128)(2,1)S(1)}, u32[]{:S(2)}, u32[]{:S(2)}) collective-permute-start(bf16[8,6144]{1,0:T(8,128)(2,1)S(1)} %fusion.33), channel_id=1, source_target_pairs={{0,40},{1,41},{2,42},{3,43},{4,44},{5,45},{6,46},{7,47},{8,32},{9,... | collective-permute-start | bytes 294920 | tf_op jit(solution)/shard_map/ppermute | solution.py:93
  78.0 7.1 %collective-permute-start.11 = (bf16[8,6144]{1,0:T(8,128)(2,1)S(1)}, bf16[8,6144]{1,0:T(8,128)(2,1)S(1)}, u32[]{:S(2)}, u32[]{:S(2)}) collective-permute-start(bf16[8,6144]{1,0:T(8,128)(2,1)S(1)} %get-tuple-element.47), channel_id=1, source_target_pairs={{0,24},{1,25},{2,26},{3,27},{4,28},{5,29},{6,30},{7,31},{8,48},{9,... | collective-permute-start | bytes 294920 | tf_op jit(solution)/shard_map/ppermute | solution.py:93
  79.7 8.5 %collective-permute-start.19 = (bf16[8,6144]{1,0:T(8,128)(2,1)S(1)}, bf16[8,6144]{1,0:T(8,128)(2,1)S(1)}, u32[]{:S(2)}, u32[]{:S(2)}) collective-permute-start(bf16[8,6144]{1,0:T(8,128)(2,1)S(1)} %get-tuple-element.46), channel_id=1, source_target_pairs={{0,40},{1,41},{2,42},{3,43},{4,44},{5,45},{6,46},{7,47},{8,32},{9,... | collective-permute-start | bytes 294920 | tf_op jit(solution)/shard_map/ppermute | solution.py:93
  92.9 8.2 %collective-permute-start.21 = (bf16[32,6144]{1,0:T(8,128)(2,1)S(1)}, bf16[32,6144]{1,0:T(8,128)(2,1)S(1)}, u32[]{:S(2)}, u32[]{:S(2)}) collective-permute-start(bf16[32,6144]{1,0:T(8,128)(2,1)S(1)} %pad_maximum_fusion.6), channel_id=1, source_target_pairs={{0,56},{1,193},{2,58},{3,195},{4,60},{5,197},{6,62},{7,199},{8,16}... | collective-permute-start | bytes 1179656 | tf_op jit(solution)/shard_map/ppermute | solution.py:93
  98.0 22.5 %collective-permute-start.14 = (bf16[64,6144]{1,0:T(8,128)(2,1)S(1)}, bf16[64,6144]{1,0:T(8,128)(2,1)S(1)}, u32[]{:S(2)}, u32[]{:S(2)}) collective-permute-start(bf16[64,6144]{1,0:T(8,128)(2,1)S(1)} %pad_maximum_fusion.2), channel_id=1, source_target_pairs={{0,192},{1,57},{2,194},{3,59},{4,196},{5,61},{6,198},{7,63},{8,200... | collective-permute-start | bytes 2359304 | tf_op jit(solution)/shard_map/ppermute | solution.py:93
  101.2 19.4 %collective-permute-start.22 = (bf16[64,6144]{1,0:T(8,128)(2,1)S(1)}, bf16[64,6144]{1,0:T(8,128)(2,1)S(1)}, u32[]{:S(2)}, u32[]{:S(2)}) collective-permute-start(bf16[64,6144]{1,0:T(8,128)(2,1)S(1)} %pad_maximum_fusion.3), channel_id=1, source_target_pairs={{0,64},{1,9},{2,66},{3,11},{4,68},{5,13},{6,70},{7,15},{8,72},{9,1... | collective-permute-start | bytes 2359304 | tf_op jit(solution)/shard_map/ppermute | solution.py:93
  105.9 14.6 %collective-permute-start.25 = (bf16[2,256,384]{2,1,0:T(8,128)(2,1)S(1)}, bf16[2,256,384]{2,1,0:T(8,128)(2,1)S(1)}, u32[]{:S(2)}, u32[]{:S(2)}) collective-permute-start(bf16[2,256,384]{2,1,0:T(8,128)(2,1)S(1)} %pad_maximum_fusion.7), channel_id=1, source_target_pairs={{0,1},{1,0},{2,3},{3,2},{4,5},{5,4},{6,7},{7,6},{8,9},{9,8},{10,11... | collective-permute-start | bytes 1179656 | tf_op jit(solution)/shard_map/ppermute | solution.py:31
  120.9 19.9 %collective-permute-start.23 = (bf16[128,6144]{1,0:T(8,128)(2,1)S(1)}, bf16[128,6144]{1,0:T(8,128)(2,1)S(1)}, u32[]{:S(2)}, u32[]{:S(2)}) collective-permute-start(bf16[128,6144]{1,0:T(8,128)(2,1)S(1)} %constant_dynamic-update-slice_fusion.a_ref), channel_id=1, source_target_pairs={{0,64},{1,9},{2,66},{3,11},{4,68},{5,13},{6,70},{7,15},{8,72},{9,1... | collective-permute-start | bytes 4718600 | tf_op jit(solution)/shard_map/ppermute | solution.py:93
  122.7 20.8 %collective-permute-start.24 = (bf16[128,6144]{1,0:T(8,128)(2,1)S(1)}, bf16[128,6144]{1,0:T(8,128)(2,1)S(1)}, u32[]{:S(2)}, u32[]{:S(2)}) collective-permute-start(bf16[128,6144]{1,0:T(8,128)(2,1)S(1)} %constant_dynamic-update-slice_fusion.5.h_ref), channel_id=1, source_target_pairs={{0,192},{1,57},{2,194},{3,59},{4,196},{5,61},{6,198},{7,63},{8,200... | collective-permute-start | bytes 4718600 | tf_op jit(solution)/shard_map/ppermute | solution.py:93
  128.3 32.3 %collective-permute-start.27 = (bf16[2,128,3072]{2,1,0:T(8,128)(2,1)S(1)}, bf16[2,128,3072]{2,1,0:T(8,128)(2,1)S(1)}, u32[]{:S(2)}, u32[]{:S(2)}) collective-permute-start(bf16[2,128,3072]{2,1,0:T(8,128)(2,1)S(1)} %pad_maximum_fusion.1), channel_id=1, source_target_pairs={{0,1},{1,0},{2,3},{3,2},{4,5},{5,4},{6,7},{7,6},{8,9},{9,8},{10,11... | collective-permute-start | bytes 4718600 | tf_op jit(solution)/shard_map/ppermute | solution.py:31
  143.9 16.8 %collective-permute-start.26 = (bf16[2,128,3072]{2,1,0:T(8,128)(2,1)S(1)}, bf16[2,128,3072]{2,1,0:T(8,128)(2,1)S(1)}, u32[]{:S(2)}, u32[]{:S(2)}) collective-permute-start(bf16[2,128,3072]{2,1,0:T(8,128)(2,1)S(1)} %pad_maximum_fusion), channel_id=1, source_target_pairs={{0,1},{1,0},{2,3},{3,2},{4,5},{5,4},{6,7},{7,6},{8,9},{9,8},{10,11... | collective-permute-start | bytes 4718600 | tf_op jit(solution)/shard_map/ppermute | solution.py:31
  158.5 8.1 %collective-permute-start.30 = (bf16[2,64,384]{2,1,0:T(8,128)(2,1)S(1)}, bf16[2,64,384]{2,1,0:T(8,128)(2,1)S(1)}, u32[]{:S(2)}, u32[]{:S(2)}) collective-permute-start(bf16[2,64,384]{2,1,0:T(8,128)(2,1)S(1)} %get-tuple-element.58), channel_id=1, source_target_pairs={{0,6},{1,7},{2,0},{3,1},{4,2},{5,3},{6,4},{7,5},{8,14},{9,15},{10,... | collective-permute-start | bytes 294920 | tf_op jit(solution)/shard_map/ppermute | solution.py:27
  159.3 7.3 %collective-permute-start.29 = (bf16[2,64,384]{2,1,0:T(8,128)(2,1)S(1)}, bf16[2,64,384]{2,1,0:T(8,128)(2,1)S(1)}, u32[]{:S(2)}, u32[]{:S(2)}) collective-permute-start(bf16[2,64,384]{2,1,0:T(8,128)(2,1)S(1)} %get-tuple-element.59), channel_id=1, source_target_pairs={{0,4},{1,5},{2,6},{3,7},{4,0},{5,1},{6,2},{7,3},{8,12},{9,13},{10,... | collective-permute-start | bytes 294920 | tf_op jit(solution)/shard_map/ppermute | solution.py:27
  160.0 7.6 %collective-permute-start.28 = (bf16[2,64,384]{2,1,0:T(8,128)(2,1)S(1)}, bf16[2,64,384]{2,1,0:T(8,128)(2,1)S(1)}, u32[]{:S(2)}, u32[]{:S(2)}) collective-permute-start(bf16[2,64,384]{2,1,0:T(8,128)(2,1)S(1)} %get-tuple-element.57), channel_id=1, source_target_pairs={{0,2},{1,3},{2,4},{3,5},{4,6},{5,7},{6,0},{7,1},{8,10},{9,11},{10,... | collective-permute-start | bytes 294920 | tf_op jit(solution)/shard_map/ppermute | solution.py:27
  (11 other events, 44.2 us)
